TPU v7x, 32 devices: a whole 2x2x4 slice. The times are simulated.
32 devices in a mesh: grp: 2 (over y), fsdp: 8 (over z, x), seq: 2 (over core).
Axes of the slice: x: 2, y: 2, z: 4, core: 2. Of those that a mesh axis runs over, the one named last changes fastest.
Arguments:
- image_tokens: bfloat16 [16, 512, 3072], P(('grp', 'fsdp'), 'seq'), parts along dimension 0, may hold values from -6 to 6
- adjoint: bfloat16 [16, 512, 3072], P(('grp', 'fsdp'), 'seq'), parts along dimension 0, may hold values from -24 to 24
- attn_keys: bfloat16 [16, 768, 1536], P(('grp', 'fsdp'), 'seq'), parts along dimension 0, may hold values from -2.5 to 2.5
- attn_values: bfloat16 [16, 768, 1536], P(('grp', 'fsdp'), 'seq'), parts along dimension 0, may hold values from -6 to 6
- w_query: bfloat16 [3072, 1536], P('fsdp', 'seq'), may hold values from -0.109375 to 0.109375
- w_out: bfloat16 [1536, 3072], P('seq', 'fsdp'), may hold values from -0.15625 to 0.15625
- q_gain: float32 [128], replicated, may hold values from 1 to 2.5
- mod_table: float32 [28, 3, 3072], replicated, may hold values from -4 to 4
- timesteps: int32 [16], P(('grp', 'fsdp')), parts along dimension 0, may hold values from 0 to 27
- text_counts: int32 [16], P(('grp', 'fsdp')), parts along dimension 0, may hold values from 1 to 256
Outputs:
- branch_cotangent: float32 [16, 512, 3072], P(('grp', 'fsdp'), 'seq'), parts along dimension 0
There are 2 independent parts, one for each index of `grp`. A program takes and returns all parts, laid end to end along the dimension named above; an argument that names none is the same for every part. Nothing has to cross between parts.
Inputs may be any that keep to these rules, and one draw needn't show every extreme that they name: Of a prompt's 256 text keys, the first text_counts of them are real and the rest are padding.
All inputs are finite; a program needn't handle non-finite values.
Results may differ from a plain program's by a relative error of at most 0.0092.
Values may be sent and summed in bfloat16 or wider, within the bound.
A program may use at most 128 MiB of HBM per device.

v0:
```python
import jax
import jax.numpy as jnp
from jax import lax
from jax.sharding import PartitionSpec as P

HD = 128
SWAP = ((0, 1), (1, 0))


def contract_last(left, right):
    return lax.dot_general(
        left, right, (((1,), (1,)), ((), ())), preferred_element_type=jnp.float32
    )


def swap(piece):
    return lax.ppermute(piece, "seq", SWAP)


def local(
    image_tokens,
    adjoint,
    attn_keys,
    attn_values,
    w_query,
    w_out,
    q_gain,
    mod_table,
    timesteps,
    text_counts,
):
    me = lax.axis_index("seq")
    half = w_query.shape[1]
    heads = half // HD
    factor = HD ** (-0.5)
    w_q = lax.all_gather(w_query, "fsdp", axis=0, tiled=True)
    w_o = lax.all_gather(w_out.T, "fsdp", axis=0, tiled=True)
    modulation = lax.dynamic_index_in_dim(mod_table, timesteps[0], 0, keepdims=False)
    shift_row, scale_row, gate_row = (modulation[0], modulation[1], modulation[2])
    tokens = image_tokens[0].astype(jnp.float32)
    mean = jnp.mean(tokens, axis=-1, keepdims=True)
    centred = tokens - mean
    inv = lax.rsqrt(jnp.mean(centred * centred, axis=-1, keepdims=True) + 1e-06)
    normed = (centred * inv * (1.0 + scale_row) + shift_row).astype(jnp.bfloat16)
    d_branch = (gate_row * adjoint[0].astype(jnp.float32)).astype(jnp.bfloat16)

    def halves(rows):
        own = lax.dynamic_slice_in_dim(rows, me * half, half, 1)
        other = lax.dynamic_slice_in_dim(rows, (1 - me) * half, half, 1)
        return jnp.concatenate([own, swap(other)], axis=0)

    keys, values = (halves(attn_keys[0]), halves(attn_values[0]))
    key_rows = attn_keys.shape[1]
    txt = keys.shape[0] // 3
    spots = jnp.arange(key_rows, dtype=jnp.int32)
    positions = jnp.concatenate([me * key_rows + spots, (1 - me) * key_rows + spots])
    usable = (positions >= txt) | (positions < text_counts[0])
    normed_all = jnp.concatenate([normed, swap(normed)], axis=0)
    d_branch_all = jnp.concatenate([d_branch, swap(d_branch)], axis=0)
    query = jnp.dot(normed_all, w_q, preferred_element_type=jnp.float32)
    d_attn = jnp.dot(d_branch_all, w_o, preferred_element_type=jnp.float32).astype(jnp.bfloat16)
    parts = []
    for head in range(heads):
        cols = slice(head * HD, (head + 1) * HD)
        q_head, k_head, v_head = (query[:, cols], keys[:, cols], values[:, cols])
        root = lax.rsqrt(jnp.mean(q_head * q_head, axis=-1, keepdims=True) + 1e-06)
        unit = q_head * root
        q_normed = (unit * q_gain).astype(jnp.bfloat16)
        scores = contract_last(q_normed, k_head) * factor
        terms = jnp.where(usable[None, :], jnp.exp(scores), 0.0)
        probs = terms / jnp.sum(terms, axis=-1, keepdims=True)
        d_probs = contract_last(d_attn[:, cols], v_head)
        centre = jnp.sum(probs * d_probs, axis=-1, keepdims=True)
        d_scores = (probs * (d_probs - centre) * factor).astype(jnp.bfloat16)
        d_unit = jnp.dot(d_scores, k_head, preferred_element_type=jnp.float32) * q_gain
        d_query = root * (d_unit - unit * jnp.mean(d_unit * unit, axis=-1, keepdims=True))
        parts.append(d_query.astype(jnp.bfloat16))
    d_query = jnp.concatenate(parts, axis=1)
    count = tokens.shape[0]
    theirs = contract_last(d_query[count:], w_q).astype(jnp.bfloat16)
    mine = contract_last(d_query[:count], w_q)
    d_normed = mine + swap(theirs).astype(jnp.float32)
    d_hat = d_normed * (1.0 + scale_row)
    hat = centred * inv
    d_mean = jnp.mean(d_hat, axis=-1, keepdims=True)
    d_proj = jnp.mean(d_hat * hat, axis=-1, keepdims=True)
    return (inv * (d_hat - d_mean - hat * d_proj))[None]


def solution(mesh):
    in_specs = (
        P(("grp", "fsdp"), "seq", None),
        P(("grp", "fsdp"), "seq", None),
        P(("grp", "fsdp"), "seq", None),
        P(("grp", "fsdp"), "seq", None),
        P("fsdp", "seq"),
        P("seq", "fsdp"),
        P(),
        P(),
        P(("grp", "fsdp")),
        P(("grp", "fsdp")),
    )
    out_specs = P(("grp", "fsdp"), "seq", None)
    return jax.shard_map(local, mesh=mesh, in_specs=in_specs, out_specs=out_specs, check_vma=False)
```

profile of v0, /device:TPU:0, one launch (start us, length us, event | category | flops | bytes accessed | tf_op | source)
XLA Modules:
  0.0 214.6 jit_solution(10942834821170242803)
XLA Ops:
  6.5 0.7 all-gather.3.cloned.1.call-update
  7.3 0.7 all-gather.5.cloned.1.call-update
  8.7 1.7 convert_reduce_fusion
  10.4 0.6 fusion.12
  11.0 1.0 constant_dynamic-slice_fusion
  12.0 1.9 fusion.7
  13.9 0.5 collective-permute-start
  14.4 0.9 dynamic-slice_bitcast_fusion.2
  15.3 0.5 copy-done.10
  15.9 0.9 dynamic-slice_bitcast_fusion
  16.8 1.5 fusion.21
  18.3 0.5 collective-permute-start.2
  19.5 72.7 %all-gather.3.cloned.1.call-done = bf16[3072,768]{1,0:T(8,128)(2,1)} async-done(((bf16[384,768]{1,0:T(8,128)(2,1)}), bf16[3072,768]{1,0:T(8,128)(2,1)}) %all-gather.3.cloned.1.call-update) | async-done | bytes 4718608 | tf_op jit(solution)/shard_map/all_gather | solution.py:36
  92.2 5.9 %fusion.13 = f32[512,768]{1,0:T(8,128)S(1)} fusion(bf16[3072,768]{1,0:T(8,128)(2,1)} %all-gather.3.cloned.1.call-done, bf16[256,3072]{1,0:T(8,128)(2,1)} %collective-permute-done, bf16[256,3072]{1,0:T(8,128)(2,1)} %fusion.7), kind=kOutput, calls=%fused_computation.16 | convolution fusion | flops 2422210560 | bytes 9437184 | tf_op jit(solution)/shard_map/dot_general | solution.py:60
  98.1 0.5 multiply_reduce_fusion.7
  98.7 2.2 %fusion.116 = (f32[512]{0:T(512)}, f32[512,768]{1,0:T(8,128)}) fusion(bf16[384,768]{1,0:T(8,128)(2,1)S(1)} %get-tuple-element.20, bf16[384,768]{1,0:T(8,128)(2,1)S(1)} %collective-permute-done.1, f32[512,768]{1,0:T(8,128)S(1)} %fusion.13, f32[512]{0:T(512)S(1)} %get-tuple-element.56, f32[128]{0:T(128)S(1)} %copy-done.23, pred[768]{0:T(1024)(128)(4,1)S(1)} %compare_or_fusion), kind=kOutput, calls=%fused_computation.213 | convolution fusion | flops 102432256 | bytes 3020288 | tf_op jit(solution)/shard_map/dot_general | solution.py:11
  101.0 2.2 %fusion.111 = (f32[512]{0:T(512)}, f32[512,768]{1,0:T(8,128)}) fusion(bf16[384,768]{1,0:T(8,128)(2,1)S(1)} %get-tuple-element.20, bf16[384,768]{1,0:T(8,128)(2,1)S(1)} %collective-permute-done.1, f32[512,768]{1,0:T(8,128)S(1)} %fusion.13, f32[128]{0:T(128)S(1)} %copy-done.23, f32[512]{0:T(512)S(1)} %get-tuple-element.57, pred[768]{0:T(1024)(128)(4,1)S(1)} %compare_or_fusion), kind=kOutput, calls=%fused_computation.208 | convolution fusion | flops 102432256 | bytes 3020288 | tf_op jit(solution)/shard_map/dot_general | solution.py:11
  103.2 2.3 %fusion.114 = (f32[512]{0:T(512)}, f32[512,768]{1,0:T(8,128)}) fusion(bf16[384,768]{1,0:T(8,128)(2,1)S(1)} %get-tuple-element.20, bf16[384,768]{1,0:T(8,128)(2,1)S(1)} %collective-permute-done.1, f32[512,768]{1,0:T(8,128)S(1)} %fusion.13, f32[512]{0:T(512)S(1)} %get-tuple-element.54, f32[128]{0:T(128)S(1)} %copy-done.23, pred[768]{0:T(1024)(128)(4,1)S(1)} %compare_or_fusion), kind=kOutput, calls=%fused_computation.211 | convolution fusion | flops 102432256 | bytes 3020288 | tf_op jit(solution)/shard_map/dot_general | solution.py:11
  105.5 2.2 %fusion.115 = (f32[512]{0:T(512)}, f32[512,768]{1,0:T(8,128)}) fusion(bf16[384,768]{1,0:T(8,128)(2,1)S(1)} %get-tuple-element.20, bf16[384,768]{1,0:T(8,128)(2,1)S(1)} %collective-permute-done.1, f32[512,768]{1,0:T(8,128)S(1)} %fusion.13, f32[512]{0:T(512)S(1)} %get-tuple-element.55, f32[128]{0:T(128)S(1)} %copy-done.23, pred[768]{0:T(1024)(128)(4,1)S(1)} %compare_or_fusion), kind=kOutput, calls=%fused_computation.212 | convolution fusion | flops 102432256 | bytes 3020288 | tf_op jit(solution)/shard_map/dot_general | solution.py:11
  107.7 2.2 %fusion.113 = (f32[512]{0:T(512)}, f32[512,768]{1,0:T(8,128)}) fusion(bf16[384,768]{1,0:T(8,128)(2,1)S(1)} %get-tuple-element.20, bf16[384,768]{1,0:T(8,128)(2,1)S(1)} %collective-permute-done.1, f32[512,768]{1,0:T(8,128)S(1)} %fusion.13, f32[512]{0:T(512)S(1)} %get-tuple-element.53, f32[128]{0:T(128)S(1)} %copy-done.23, pred[768]{0:T(1024)(128)(4,1)S(1)} %compare_or_fusion), kind=kOutput, calls=%fused_computation.210 | convolution fusion | flops 102432256 | bytes 3020288 | tf_op jit(solution)/shard_map/dot_general | solution.py:11
  109.9 2.2 %fusion.112 = (f32[512]{0:T(512)}, f32[512,768]{1,0:T(8,128)}) fusion(bf16[768,128]{1,0:T(8,128)(2,1)S(1)} %pad_maximum_fusion.2, f32[512,768]{1,0:T(8,128)S(1)} %fusion.13, f32[512]{0:T(512)S(1)} %get-tuple-element.52, f32[128]{0:T(128)S(1)} %copy-done.23, pred[768]{0:T(1024)(128)(4,1)S(1)} %compare_or_fusion), kind=kOutput, calls=%fused_computation.209 | convolution fusion | flops 102039040 | bytes 2037248 | tf_op jit(solution)/shard_map/dot_general | solution.py:11
  112.1 61.2 %all-gather.5.cloned.1.call-done = bf16[3072,768]{0,1:T(8,128)(2,1)} async-done(((bf16[384,768]{0,1:T(8,128)(2,1)}), bf16[3072,768]{0,1:T(8,128)(2,1)}) %all-gather.5.cloned.1.call-update) | async-done | bytes 4718608 | tf_op jit(solution)/shard_map/all_gather | solution.py:37
  173.4 6.0 %fusion.22 = bf16[512,768]{1,0:T(8,128)(2,1)S(1)} fusion(bf16[3072,768]{0,1:T(8,128)(2,1)} %all-gather.5.cloned.1.call-done, bf16[256,3072]{1,0:T(8,128)(2,1)} %collective-permute-done.2, bf16[256,3072]{1,0:T(8,128)(2,1)} %fusion.21), kind=kOutput, calls=%fused_computation.65 | convolution fusion | flops 2422603776 | bytes 8650752 | tf_op jit(solution)/shard_map/dot_general | solution.py:61
  179.5 1.4 multiply_reduce_fusion.4
  180.9 0.5 convolution_multiply_fusion.4
  181.4 0.9 copy-done.8
  182.3 1.4 multiply_reduce_fusion.5
  183.7 0.5 convolution_multiply_fusion.5
  184.2 0.9 copy-done.6
  185.1 1.4 multiply_reduce_fusion.2
  186.5 0.7 convolution_multiply_fusion.2
  187.1 0.7 copy-done.5
  187.9 1.4 multiply_reduce_fusion.3
  189.2 0.5 convolution_multiply_fusion.3
  189.7 0.9 copy-done.4
  190.6 1.5 multiply_reduce_fusion.1
  192.1 1.4 multiply_reduce_fusion
  193.6 0.5 convolution_multiply_fusion.1
  194.1 0.8 copy-done.2
  195.0 1.2 multiply_reduce_fusion.6
  196.4 0.3 fusion.64
  196.9 0.3 fusion.66
  197.2 0.3 fusion.67
  197.4 0.3 fusion.68
  197.8 1.4 convolution_convert_fusion
  199.3 3.4 %collective-permute-done.4 = bf16[256,3072]{1,0:T(8,128)(2,1)S(1)} collective-permute-done((bf16[256,3072]{1,0:T(8,128)(2,1)S(1)}, bf16[256,3072]{1,0:T(8,128)(2,1)S(1)}, u32[]{:S(2)}, u32[]{:S(2)}) %collective-permute-start.4) | collective-permute-done | bytes 1572896 | tf_op jit(solution)/shard_map/ppermute | solution.py:17
  202.7 2.0 fusion.25
  204.7 3.0 %fusion.11 = f32[1,256,3072]{2,1,0:T(8,128)} fusion(bf16[1,256,3072]{2,1,0:T(8,128)(2,1)S(1)} %copy-done, f32[256]{0:T(256)S(1)} %broadcast_multiply_fusion.6, f32[256]{0:T(256)S(1)} %broadcast_multiply_fusion.7, f32[256]{0:T(256)S(1)} %copy-done.26, f32[256]{0:T(256)S(1)} %copy-done.22, f32[3072]{0:T(1024)S(1)} %bitcast.60, ...), kind=kLoop, calls=%fused_computation.14 | loop fusion | flops 7864320 | bytes 9453568 | tf_op jit(solution)/shard_map/broadcast_in_dim | solution.py:87
  (98 shorter events, 1.0 us)
Async XLA Ops:
  6.5 3.8 %copy-start = (bf16[1,256,3072]{2,1,0:T(8,128)(2,1)S(1)}, bf16[1,256,3072]{2,1,0:T(8,128)(2,1)}, u32[]{:S(2)}) copy-start(bf16[1,256,3072]{2,1,0:T(8,128)(2,1)} %param.10) | copy-start | bytes 4718596
  6.5 85.6 %all-gather.3.cloned.1.call-start = ((), (), s32[]{:S(2)}) async-start(), calls=%async_computation | async-start | bytes 5308416 | tf_op jit(solution)/shard_map/all_gather | solution.py:36
  7.3 166.1 %all-gather.5.cloned.1.call-start = ((), (), s32[]{:S(2)}) async-start(), calls=%async_computation.1 | async-start | bytes 5308416 | tf_op jit(solution)/shard_map/all_gather | solution.py:37
  10.4 3.6 %copy-start.21 = (f32[256]{0:T(256)}, f32[256]{0:T(256)S(1)}, u32[]{:S(2)}) copy-start(f32[256]{0:T(256)S(1)} %broadcast_multiply_fusion.8) | copy-start | bytes 3076
  10.9 3.0 %copy-start.25 = (f32[256]{0:T(256)}, f32[256]{0:T(256)S(1)}, u32[]{:S(2)}) copy-start(f32[256]{0:T(256)S(1)} %add_rsqrt_fusion.6) | copy-start | bytes 3076
  12.0 2.4 %copy-start.9 = (bf16[1,384,1536]{2,1,0:T(8,128)(2,1)S(1)}, bf16[1,384,1536]{2,1,0:T(8,128)(2,1)}, u32[]{:S(2)}) copy-start(bf16[1,384,1536]{2,1,0:T(8,128)(2,1)} %param.12) | copy-start | bytes 3538948
  13.9 5.5 %collective-permute-start = (bf16[256,3072]{1,0:T(8,128)(2,1)}, bf16[256,3072]{1,0:T(8,128)(2,1)}, u32[]{:S(2)}, u32[]{:S(2)}) collective-permute-start(bf16[256,3072]{1,0:T(8,128)(2,1)} %fusion.7), channel_id=1, source_target_pairs={{0,1},{1,0},{2,3},{3,2},{4,5},{5,4},{6,7},{7,6},{8,9},{9,8},{10,11... | collective-permute-start | bytes 4718600 | tf_op jit(solution)/shard_map/ppermute | solution.py:17
  14.4 1.5 copy-start.10
  15.3 1.6 copy-start.3
  15.3 4.2 %collective-permute-start.1 = (bf16[384,768]{1,0:T(8,128)(2,1)}, bf16[384,768]{1,0:T(8,128)(2,1)S(1)}, u32[]{:S(2)}, u32[]{:S(2)}) collective-permute-start(bf16[384,768]{1,0:T(8,128)(2,1)} %get-tuple-element.19), channel_id=1, source_target_pairs={{0,1},{1,0},{2,3},{3,2},{4,5},{5,4},{6,7},{7,6},{8,9},{9,8},{10,11... | collective-permute-start | bytes 1769480 | tf_op jit(solution)/shard_map/ppermute | solution.py:17
  16.8 162.7 %collective-permute-start.3 = (bf16[384,768]{1,0:T(8,128)(2,1)}, bf16[384,768]{1,0:T(8,128)(2,1)}, u32[]{:S(2)}, u32[]{:S(2)}) collective-permute-start(bf16[384,768]{1,0:T(8,128)(2,1)} %get-tuple-element.24), channel_id=1, source_target_pairs={{0,1},{1,0},{2,3},{3,2},{4,5},{5,4},{6,7},{7,6},{8,9},{9,8},{10,11... | collective-permute-start | bytes 1769480 | tf_op jit(solution)/shard_map/ppermute | solution.py:17
  18.3 93.9 %collective-permute-start.2 = (bf16[256,3072]{1,0:T(8,128)(2,1)}, bf16[256,3072]{1,0:T(8,128)(2,1)}, u32[]{:S(2)}, u32[]{:S(2)}) collective-permute-start(bf16[256,3072]{1,0:T(8,128)(2,1)} %fusion.21), channel_id=1, source_target_pairs={{0,1},{1,0},{2,3},{3,2},{4,5},{5,4},{6,7},{7,6},{8,9},{9,8},{10,11... | collective-permute-start | bytes 4718600 | tf_op jit(solution)/shard_map/ppermute | solution.py:17
  98.1 11.8 %copy-start.1 = (f32[512,768]{1,0:T(8,128)}, f32[512,768]{1,0:T(8,128)S(1)}, u32[]{:S(2)}) copy-start(f32[512,768]{1,0:T(8,128)S(1)} %fusion.13) | copy-start | bytes 4718596
  98.1 0.7 copy-start.23
  98.6 9.1 %copy-start.11 = (f32[512]{0:T(512)}, f32[512]{0:T(512)S(1)}, u32[]{:S(2)}) copy-start(f32[512]{0:T(512)S(1)} %get-tuple-element.53) | copy-start | bytes 6148
  98.6 11.3 %copy-start.27 = (f32[512]{0:T(512)}, f32[512]{0:T(512)S(1)}, u32[]{:S(2)}) copy-start(f32[512]{0:T(512)S(1)} %get-tuple-element.52) | copy-start | bytes 6148
  98.6 2.3 %copy-start.15 = (f32[512]{0:T(512)}, f32[512]{0:T(512)S(1)}, u32[]{:S(2)}) copy-start(f32[512]{0:T(512)S(1)} %get-tuple-element.56) | copy-start | bytes 6148
  98.6 4.6 %copy-start.17 = (f32[512]{0:T(512)}, f32[512]{0:T(512)S(1)}, u32[]{:S(2)}) copy-start(f32[512]{0:T(512)S(1)} %get-tuple-element.57) | copy-start | bytes 6148
  101.0 4.5 %copy-start.13 = (f32[512]{0:T(512)}, f32[512]{0:T(512)S(1)}, u32[]{:S(2)}) copy-start(f32[512]{0:T(512)S(1)} %get-tuple-element.54) | copy-start | bytes 6148
  101.0 4.5 %copy-start.19 = (f32[512]{0:T(512)}, f32[512]{0:T(512)S(1)}, u32[]{:S(2)}) copy-start(f32[512]{0:T(512)S(1)} %get-tuple-element.55) | copy-start | bytes 6148
  112.1 67.3 %copy-start.32 = (f32[512]{0:T(512)S(1)}, f32[512]{0:T(512)}, u32[]{:S(2)}) copy-start(f32[512]{0:T(512)} %get-tuple-element.46) | copy-start | bytes 6148
  173.4 6.1 %copy-start.7 = (f32[512,768]{1,0:T(8,128)S(1)}, f32[512,768]{1,0:T(8,128)}, u32[]{:S(2)}) copy-start(f32[512,768]{1,0:T(8,128)} %get-tuple-element.47) | copy-start | bytes 4718596
  179.5 1.4 copy-start.24
  180.9 1.4 copy-start.8
  180.9 1.4 copy-start.33
  183.7 1.4 copy-start.6
  183.7 1.4 copy-start.31
  186.4 1.4 copy-start.5
  186.4 1.4 copy-start.30
  189.2 1.4 copy-start.4
  189.2 1.4 copy-start.29
  190.6 1.5 copy-start.34
  190.6 1.5 copy-start.35
  193.5 1.4 copy-start.2
  193.5 1.4 copy-start.12
  193.5 1.4 copy-start.14
  193.5 1.4 copy-start.16
  193.5 1.4 copy-start.18
  193.6 1.4 copy-start.20
  193.6 1.4 copy-start.28
  193.6 4.1 %slice-start = ((s8[4718592]{0:T(1024)(128)(4,1)}), s8[4194304]{0:T(1024)(128)(4,1)S(1)}, s32[]{:S(2)}) async-start(s8[4718592]{0:T(1024)(128)(4,1)} %bitcast.63), calls=%async_computation.2 | async-start | bytes 8388608
  195.0 2.8 %slice-start.1 = ((s8[4718592]{0:T(1024)(128)(4,1)}), s8[524288]{0:T(1024)(128)(4,1)S(1)}, s32[]{:S(2)}) async-start(s8[4718592]{0:T(1024)(128)(4,1)} %bitcast.63), calls=%async_computation.3 | async-start | bytes 1048576
  197.7 4.9 %copy-start.22 = (f32[256]{0:T(256)S(1)}, f32[256]{0:T(256)}, u32[]{:S(2)}) copy-start(f32[256]{0:T(256)} %copy-done.21) | copy-start | bytes 3076
  197.7 4.9 %copy-start.26 = (f32[256]{0:T(256)S(1)}, f32[256]{0:T(256)}, u32[]{:S(2)}) copy-start(f32[256]{0:T(256)} %copy-done.25) | copy-start | bytes 3076
  199.2 3.5 %collective-permute-start.4 = (bf16[256,3072]{1,0:T(8,128)(2,1)S(1)}, bf16[256,3072]{1,0:T(8,128)(2,1)S(1)}, u32[]{:S(2)}, u32[]{:S(2)}) collective-permute-start(bf16[256,3072]{1,0:T(8,128)(2,1)S(1)} %convolution_convert_fusion), channel_id=1, source_target_pairs={{0,1},{1,0},{2,3},{3,2},{4,5},{5,4},{6,7},{7,6},{8,9},{9,8},{10,11... | collective-permute-start | bytes 4718600 | tf_op jit(solution)/shard_map/ppermute | solution.py:17
Sparse Core Ops, SparseCore 0:
  9.5 82.5 all-gather.2
  94.2 79.1 all-gather.4
where the time goes:
time: 215 us
  waiting for transfers between devices  139 us (65%)
  matrix products  40.9 us (19%)
  between operations  15.3 us (7%)
  other arithmetic  11.8 us (5%)
  local copies, waits for them, and re-layouts  6.78 us (3%)
    all_gather x1, waiting for transfers between devices, local(): w_q = lax.all_gather(w_query, 'fsdp', axis=0, tiled=True)  72.7 us
    all_gather x1, waiting for transfers between devices, local(): w_o = lax.all_gather(w_out.T, 'fsdp', axis=0, tiled=True)  61.2 us
    dot_general x14, matrix products, contract_last(): lax.dot_general(left, right, (((1,), (1,)), ((), ())), preferred_element_...  25.1 us
    dot_general x1, matrix products, local(): jnp.dot(d_branch_all, w_o, preferred_element_type=jnp.float32)  6.04 us
    dot_general x1, matrix products, local(): query = jnp.dot(normed_all, w_q, preferred_element_type=jnp.float32)  5.89 us
    unnamed x76, local copies, waits for them, and re-layouts  5.01 us
  transfers between devices with their start and end apart: 7, of which 3 were waited for; matrix products, arithmetic and copies ran while one was open for 16% of the time, Pallas kernels for 0%

commit v1 on v0

--- a/solution.py
+++ b/solution.py
@@ -33,7 +33,23 @@
     half = w_query.shape[1]
     heads = half // HD
     factor = HD ** (-0.5)
-    w_q = lax.all_gather(w_query, "fsdp", axis=0, tiled=True)
+    ways, here, step = (lax.axis_size("fsdp"), lax.axis_index("fsdp"), w_query.shape[0])
+    lengths = [n * ways if d == 0 else n for d, n in enumerate(w_query.shape)]
+    full = lax.dynamic_update_slice_in_dim(
+        jnp.zeros(lengths, w_query.dtype), w_query, here * step, axis=0
+    )
+    going_up = going_down = w_query
+    for far in range(1, ways // 2 + 1):
+        going_up = lax.ppermute(going_up, "fsdp", [(d, (d + 1) % ways) for d in range(ways)])
+        full = lax.dynamic_update_slice_in_dim(full, going_up, (here - far) % ways * step, axis=0)
+        if 2 * far < ways:
+            going_down = lax.ppermute(
+                going_down, "fsdp", [(d, (d - 1) % ways) for d in range(ways)]
+            )
+            full = lax.dynamic_update_slice_in_dim(
+                full, going_down, (here + far) % ways * step, axis=0
+            )
+    w_q = full
     w_o = lax.all_gather(w_out.T, "fsdp", axis=0, tiled=True)
     modulation = lax.dynamic_index_in_dim(mod_table, timesteps[0], 0, keepdims=False)
     shift_row, scale_row, gate_row = (modulation[0], modulation[1], modulation[2])

time: 215 us -> 196 us (0.912)
  waiting for transfers between devices: 139 us -> 97 us
  starting transfers between devices: 1.13 us -> 19.5 us
  local copies, waits for them, and re-layouts: 6.78 us -> 12.8 us
    ppermute x0 -> x7, waiting for transfers between devices: none -> 92.9 us  [the longest x4 80.6 us: local(): lax.ppermute(going_up, 'fsdp', [(d, (d + 1) % ways) for d in range(ways)])]
    all_gather x1 -> x0, waiting for transfers between devices: 72.7 us -> none  [local(): w_q = lax.all_gather(w_query, 'fsdp', axis=0, tiled=True)]
    all_gather x1, waiting for transfers between devices: 61.2 us -> 0.01 us  [local(): w_o = lax.all_gather(w_out.T, 'fsdp', axis=0, tiled=True)]
    ppermute x0 -> x7, starting transfers between devices: none -> 18.8 us  [the longest x3 10.2 us: local(): lax.ppermute(going_down, 'fsdp', [(d, (d - 1) % ways) for d in range(ways)])]
    dynamic_update_slice x0 -> x8, local copies, waits for them, and re-layouts: none -> 3.68 us  [the longest x4 2.45 us: local(): lax.dynamic_update_slice_in_dim(full, going_up, (here - far) % ways * ste...]
    unnamed x76 -> x78, local copies, waits for them, and re-layouts: 5.01 us -> 5.58 us
  transfers between devices with their start and end apart: 7 -> 13, of which waited for: 3 -> 6; matrix products, arithmetic and copies ran while one was open for 16% -> 20% of each run, Pallas kernels for 0% -> 0%
where the time goes in v1:
time: 196 us
  waiting for transfers between devices  97 us (49%)
  matrix products  41.1 us (21%)
  starting transfers between devices  19.5 us (10%)
  between operations  15.3 us (8%)
  local copies, waits for them, and re-layouts  12.8 us (7%)
  other arithmetic  10.1 us (5%)
    ppermute x4, waiting for transfers between devices, local(): lax.ppermute(going_up, 'fsdp', [(d, (d + 1) % ways) for d in range(ways)])  80.6 us
    dot_general x14, matrix products, contract_last(): lax.dot_general(left, right, (((1,), (1,)), ((), ())), preferred_element_...  25.3 us
    ppermute x3, waiting for transfers between devices, local(): lax.ppermute(going_down, 'fsdp', [(d, (d - 1) % ways) for d in range(ways)])  12.3 us
    ppermute x3, starting transfers between devices, local(): lax.ppermute(going_down, 'fsdp', [(d, (d - 1) % ways) for d in range(ways)])  10.2 us
    ppermute x4, starting transfers between devices, local(): lax.ppermute(going_up, 'fsdp', [(d, (d + 1) % ways) for d in range(ways)])  8.59 us
    dot_general x1, matrix products, local(): query = jnp.dot(normed_all, w_q, preferred_element_type=jnp.float32)  6.18 us
    dot_general x1, matrix products, local(): jnp.dot(d_branch_all, w_o, preferred_element_type=jnp.float32)  6.07 us
    unnamed x78, local copies, waits for them, and re-layouts  5.58 us
  transfers between devices with their start and end apart: 13, of which 6 were waited for; matrix products, arithmetic and copies ran while one was open for 20% of the time, Pallas kernels for 0%

profile of v1, /device:TPU:0, one launch (start us, length us, event | category | flops | bytes accessed | tf_op | source)
XLA Modules:
  0.0 195.8 jit_solution(11499667579504784950)
XLA Ops:
  6.5 0.7 all-gather.2.cloned.1.call-update
  7.3 3.0 %collective-permute-start.1 = (bf16[384,768]{1,0:T(8,128)(2,1)}, bf16[384,768]{1,0:T(8,128)(2,1)}, u32[]{:S(2)}, u32[]{:S(2)}) collective-permute-start(bf16[384,768]{1,0:T(8,128)(2,1)} %param.14), channel_id=1, source_target_pairs={{0,2},{2,4},{4,6},{6,8},{8,10},{10,12},{12,14},{14,0},{1,3},{3,5},... | collective-permute-start | bytes 1769480 | tf_op jit(solution)/shard_map/ppermute | solution.py:43
  10.2 3.1 %collective-permute-start.2 = (bf16[384,768]{1,0:T(8,128)(2,1)}, bf16[384,768]{1,0:T(8,128)(2,1)S(1)}, u32[]{:S(2)}, u32[]{:S(2)}) collective-permute-start(bf16[384,768]{1,0:T(8,128)(2,1)} %param.14), channel_id=1, source_target_pairs={{0,14},{2,0},{4,2},{6,4},{8,6},{10,8},{12,10},{14,12},{1,15},{3,1}... | collective-permute-start | bytes 1769480 | tf_op jit(solution)/shard_map/ppermute | solution.py:46
  13.4 2.1 %dynamic-slice_bitcast_fusion.2 = (bf16[384,768]{1,0:T(8,128)(2,1)}, bf16[384,768]{1,0:T(8,128)(2,1)S(1)}) fusion(bf16[1,384,1536]{2,1,0:T(8,128)(2,1)} %param.12, s32[]{:T(128)S(6)} %select_n.103, s32[]{:T(128)S(6)} %select_n.102), kind=kLoop, calls=%fused_computation.93 | loop fusion | bytes 2359304 | tf_op jit(solution)/shard_map/dynamic_slice | solution.py:65
  16.5 0.6 fusion.13
  17.0 1.0 dynamic-slice_add_fusion
  18.1 1.9 fusion.8
  20.5 1.1 dynamic-slice_bitcast_fusion
  21.7 20.4 %collective-permute-done.1 = bf16[384,768]{1,0:T(8,128)(2,1)} collective-permute-done((bf16[384,768]{1,0:T(8,128)(2,1)}, bf16[384,768]{1,0:T(8,128)(2,1)}, u32[]{:S(2)}, u32[]{:S(2)}) %collective-permute-start.1) | collective-permute-done | bytes 589856 | tf_op jit(solution)/shard_map/ppermute | solution.py:43
  42.1 2.5 %collective-permute-start.3 = (bf16[384,768]{1,0:T(8,128)(2,1)}, bf16[384,768]{1,0:T(8,128)(2,1)}, u32[]{:S(2)}, u32[]{:S(2)}) collective-permute-start(bf16[384,768]{1,0:T(8,128)(2,1)} %collective-permute-done.1), channel_id=1, source_target_pairs={{0,2},{2,4},{4,6},{6,8},{8,10},{10,12},{12,14},{14,0},{1,3},{3,5},... | collective-permute-start | bytes 1769480 | tf_op jit(solution)/shard_map/ppermute | solution.py:43
  44.6 3.0 %collective-permute-start.4 = (bf16[384,768]{1,0:T(8,128)(2,1)S(1)}, bf16[384,768]{1,0:T(8,128)(2,1)}, u32[]{:S(2)}, u32[]{:S(2)}) collective-permute-start(bf16[384,768]{1,0:T(8,128)(2,1)S(1)} %collective-permute-done.2), channel_id=1, source_target_pairs={{0,14},{2,0},{4,2},{6,4},{8,6},{10,8},{12,10},{14,12},{1,15},{3,1}... | collective-permute-start | bytes 1769480 | tf_op jit(solution)/shard_map/ppermute | solution.py:46
  47.6 1.5 fusion.22
  49.8 21.2 %collective-permute-done.3 = bf16[384,768]{1,0:T(8,128)(2,1)} collective-permute-done((bf16[384,768]{1,0:T(8,128)(2,1)}, bf16[384,768]{1,0:T(8,128)(2,1)}, u32[]{:S(2)}, u32[]{:S(2)}) %collective-permute-start.3) | collective-permute-done | bytes 589856 | tf_op jit(solution)/shard_map/ppermute | solution.py:43
  71.0 0.7 collective-permute-start.5
  72.1 0.8 copy-done.12
  72.9 1.2 constant_dynamic-update-slice_fusion.6
  74.2 4.0 %collective-permute-start.6 = (bf16[384,768]{1,0:T(8,128)(2,1)}, bf16[384,768]{1,0:T(8,128)(2,1)S(1)}, u32[]{:S(2)}, u32[]{:S(2)}) collective-permute-start(bf16[384,768]{1,0:T(8,128)(2,1)} %collective-permute-done.4), channel_id=1, source_target_pairs={{0,14},{2,0},{4,2},{6,4},{8,6},{10,8},{12,10},{14,12},{1,15},{3,1}... | collective-permute-start | bytes 1769480 | tf_op jit(solution)/shard_map/ppermute | solution.py:46
  78.3 31.9 %collective-permute-done.5 = bf16[384,768]{1,0:T(8,128)(2,1)S(1)} collective-permute-done((bf16[384,768]{1,0:T(8,128)(2,1)}, bf16[384,768]{1,0:T(8,128)(2,1)S(1)}, u32[]{:S(2)}, u32[]{:S(2)}) %collective-permute-start.5) | collective-permute-done | bytes 589856 | tf_op jit(solution)/shard_map/ppermute | solution.py:43
  110.2 2.4 %collective-permute-start.7 = (bf16[384,768]{1,0:T(8,128)(2,1)S(1)}, bf16[384,768]{1,0:T(8,128)(2,1)S(1)}, u32[]{:S(2)}, u32[]{:S(2)}) collective-permute-start(bf16[384,768]{1,0:T(8,128)(2,1)S(1)} %collective-permute-done.5), channel_id=1, source_target_pairs={{0,2},{2,4},{4,6},{6,8},{8,10},{10,12},{12,14},{14,0},{1,3},{3,5},... | collective-permute-start | bytes 1769480 | tf_op jit(solution)/shard_map/ppermute | solution.py:43
  112.6 1.1 constant_dynamic-update-slice_fusion.4
  113.7 1.1 constant_dynamic-update-slice_fusion.3
  114.9 12.3 %collective-permute-done.6 = bf16[384,768]{1,0:T(8,128)(2,1)S(1)} collective-permute-done((bf16[384,768]{1,0:T(8,128)(2,1)}, bf16[384,768]{1,0:T(8,128)(2,1)S(1)}, u32[]{:S(2)}, u32[]{:S(2)}) %collective-permute-start.6) | collective-permute-done | bytes 589856 | tf_op jit(solution)/shard_map/ppermute | solution.py:46
  127.2 7.1 %collective-permute-done.7 = bf16[384,768]{1,0:T(8,128)(2,1)S(1)} collective-permute-done((bf16[384,768]{1,0:T(8,128)(2,1)S(1)}, bf16[384,768]{1,0:T(8,128)(2,1)S(1)}, u32[]{:S(2)}, u32[]{:S(2)}) %collective-permute-start.7) | collective-permute-done | bytes 589856 | tf_op jit(solution)/shard_map/ppermute | solution.py:43
  134.4 6.2 %fusion.14 = f32[512,768]{1,0:T(8,128)S(1)} fusion(bf16[3072,768]{1,0:T(8,128)(2,1)S(1)} %constant_dynamic-update-slice_fusion, bf16[256,3072]{1,0:T(8,128)(2,1)} %collective-permute-done, bf16[256,3072]{1,0:T(8,128)(2,1)} %fusion.8), kind=kOutput, calls=%fused_computation.18 | convolution fusion | flops 2422210560 | bytes 9437184 | tf_op jit(solution)/shard_map/dot_general | solution.py:76
  141.2 2.2 %fusion.111 = (f32[512]{0:T(512)}, f32[512,768]{1,0:T(8,128)}) fusion(bf16[384,768]{1,0:T(8,128)(2,1)S(1)} %get-tuple-element.20, bf16[384,768]{1,0:T(8,128)(2,1)S(1)} %collective-permute-done.8, f32[512,768]{1,0:T(8,128)S(1)} %fusion.14, f32[128]{0:T(128)S(1)} %copy-done.24, f32[512]{0:T(512)S(1)} %get-tuple-element.57, pred[768]{0:T(1024)(128)(4,1)S(1)} %compare_or_fusion), kind=kOutput, calls=%fused_computation.216 | convolution fusion | flops 102432256 | bytes 3020288 | tf_op jit(solution)/shard_map/dot_general | solution.py:11
  143.5 2.2 %fusion.113 = (f32[512]{0:T(512)}, f32[512,768]{1,0:T(8,128)}) fusion(bf16[384,768]{1,0:T(8,128)(2,1)S(1)} %get-tuple-element.20, bf16[384,768]{1,0:T(8,128)(2,1)S(1)} %collective-permute-done.8, f32[512,768]{1,0:T(8,128)S(1)} %fusion.14, f32[512]{0:T(512)S(1)} %get-tuple-element.53, f32[128]{0:T(128)S(1)} %copy-done.24, pred[768]{0:T(1024)(128)(4,1)S(1)} %compare_or_fusion), kind=kOutput, calls=%fused_computation.218 | convolution fusion | flops 102432256 | bytes 3020288 | tf_op jit(solution)/shard_map/dot_general | solution.py:11
  145.7 2.2 %fusion.114 = (f32[512]{0:T(512)}, f32[512,768]{1,0:T(8,128)}) fusion(bf16[384,768]{1,0:T(8,128)(2,1)S(1)} %get-tuple-element.20, bf16[384,768]{1,0:T(8,128)(2,1)S(1)} %collective-permute-done.8, f32[512,768]{1,0:T(8,128)S(1)} %fusion.14, f32[512]{0:T(512)S(1)} %get-tuple-element.54, f32[128]{0:T(128)S(1)} %copy-done.24, pred[768]{0:T(1024)(128)(4,1)S(1)} %compare_or_fusion), kind=kOutput, calls=%fused_computation.219 | convolution fusion | flops 102432256 | bytes 3020288 | tf_op jit(solution)/shard_map/dot_general | solution.py:11
  148.0 2.3 %fusion.115 = (f32[512]{0:T(512)}, f32[512,768]{1,0:T(8,128)}) fusion(bf16[384,768]{1,0:T(8,128)(2,1)S(1)} %get-tuple-element.20, bf16[384,768]{1,0:T(8,128)(2,1)S(1)} %collective-permute-done.8, f32[512,768]{1,0:T(8,128)S(1)} %fusion.14, f32[512]{0:T(512)S(1)} %get-tuple-element.55, f32[128]{0:T(128)S(1)} %copy-done.24, pred[768]{0:T(1024)(128)(4,1)S(1)} %compare_or_fusion), kind=kOutput, calls=%fused_computation.220 | convolution fusion | flops 102432256 | bytes 3020288 | tf_op jit(solution)/shard_map/dot_general | solution.py:11
  150.2 2.2 %fusion.116 = (f32[512]{0:T(512)}, f32[512,768]{1,0:T(8,128)}) fusion(bf16[384,768]{1,0:T(8,128)(2,1)S(1)} %get-tuple-element.20, bf16[384,768]{1,0:T(8,128)(2,1)S(1)} %collective-permute-done.8, f32[512,768]{1,0:T(8,128)S(1)} %fusion.14, f32[512]{0:T(512)S(1)} %get-tuple-element.56, f32[128]{0:T(128)S(1)} %copy-done.24, pred[768]{0:T(1024)(128)(4,1)S(1)} %compare_or_fusion), kind=kOutput, calls=%fused_computation.221 | convolution fusion | flops 102432256 | bytes 3020288 | tf_op jit(solution)/shard_map/dot_general | solution.py:11
  152.5 2.2 %fusion.112 = (f32[512]{0:T(512)}, f32[512,768]{1,0:T(8,128)}) fusion(bf16[768,128]{1,0:T(8,128)(2,1)S(1)} %pad_maximum_fusion.2, f32[512,768]{1,0:T(8,128)S(1)} %fusion.14, f32[512]{0:T(512)S(1)} %get-tuple-element.52, f32[128]{0:T(128)S(1)} %copy-done.24, pred[768]{0:T(1024)(128)(4,1)S(1)} %compare_or_fusion), kind=kOutput, calls=%fused_computation.217 | convolution fusion | flops 102039040 | bytes 2037248 | tf_op jit(solution)/shard_map/dot_general | solution.py:11
  154.7 6.1 %fusion.23 = bf16[512,768]{1,0:T(8,128)(2,1)S(1)} fusion(bf16[3072,768]{0,1:T(8,128)(2,1)} %all-gather.2.cloned.1.call-done, bf16[256,3072]{1,0:T(8,128)(2,1)} %collective-permute-done.9, bf16[256,3072]{1,0:T(8,128)(2,1)} %fusion.22), kind=kOutput, calls=%fused_computation.66 | convolution fusion | flops 2422603776 | bytes 8650752 | tf_op jit(solution)/shard_map/dot_general | solution.py:77
  160.9 1.4 multiply_reduce_fusion.5
  162.3 0.5 convolution_multiply_fusion.5
  162.8 0.9 copy-done.9
  163.7 1.4 multiply_reduce_fusion.1
  165.5 0.9 copy-done.8
  166.4 1.4 multiply_reduce_fusion.2
  168.3 0.9 copy-done.7
  169.2 1.4 multiply_reduce_fusion.3
  171.1 0.9 copy-done.6
  172.0 1.4 multiply_reduce_fusion.4
  173.8 0.9 copy-done.35
  174.8 1.7 multiply_reduce_fusion
  176.6 1.2 multiply_reduce_fusion.6
  179.4 1.4 convolution_convert_fusion
  180.9 3.4 %collective-permute-done.11 = bf16[256,3072]{1,0:T(8,128)(2,1)S(1)} collective-permute-done((bf16[256,3072]{1,0:T(8,128)(2,1)S(1)}, bf16[256,3072]{1,0:T(8,128)(2,1)S(1)}, u32[]{:S(2)}, u32[]{:S(2)}) %collective-permute-start.11) | collective-permute-done | bytes 1572896 | tf_op jit(solution)/shard_map/ppermute | solution.py:17
  184.3 1.9 fusion.110
  186.2 2.8 %fusion.12 = f32[1,256,3072]{2,1,0:T(8,128)} fusion(bf16[1,256,3072]{2,1,0:T(8,128)(2,1)S(1)} %copy-done, f32[256,3072]{1,0:T(8,128)S(1)} %get-tuple-element.51, f32[256]{0:T(256)S(1)} %broadcast_multiply_fusion.6, f32[256]{0:T(256)S(1)} %broadcast_multiply_fusion.7, f32[256]{0:T(256)S(1)} %copy-done.27, f32[256]{0:T(256)S(1)} %copy-done.23), kind=kLoop, calls=%fused_computation.16 | loop fusion | flops 5505024 | bytes 7868416 | tf_op jit(solution)/shard_map/broadcast_in_dim | solution.py:103
  (120 shorter events, 5.7 us)
Async XLA Ops:
  6.5 9.6 %copy-start = (bf16[1,256,3072]{2,1,0:T(8,128)(2,1)S(1)}, bf16[1,256,3072]{2,1,0:T(8,128)(2,1)}, u32[]{:S(2)}) copy-start(bf16[1,256,3072]{2,1,0:T(8,128)(2,1)} %param.10) | copy-start | bytes 4718596
  6.5 148.2 %all-gather.2.cloned.1.call-start = ((), (), s32[]{:S(2)}) async-start(), calls=%async_computation | async-start | bytes 5308416 | tf_op jit(solution)/shard_map/all_gather | solution.py:53
  7.3 34.9 %collective-permute-start.1 = (bf16[384,768]{1,0:T(8,128)(2,1)}, bf16[384,768]{1,0:T(8,128)(2,1)}, u32[]{:S(2)}, u32[]{:S(2)}) collective-permute-start(bf16[384,768]{1,0:T(8,128)(2,1)} %param.14), channel_id=1, source_target_pairs={{0,2},{2,4},{4,6},{6,8},{8,10},{10,12},{12,14},{14,0},{1,3},{3,5},... | collective-permute-start | bytes 1769480 | tf_op jit(solution)/shard_map/ppermute | solution.py:43
  10.2 34.3 %collective-permute-start.2 = (bf16[384,768]{1,0:T(8,128)(2,1)}, bf16[384,768]{1,0:T(8,128)(2,1)S(1)}, u32[]{:S(2)}, u32[]{:S(2)}) collective-permute-start(bf16[384,768]{1,0:T(8,128)(2,1)} %param.14), channel_id=1, source_target_pairs={{0,14},{2,0},{4,2},{6,4},{8,6},{10,8},{12,10},{14,12},{1,15},{3,1}... | collective-permute-start | bytes 1769480 | tf_op jit(solution)/shard_map/ppermute | solution.py:46
  15.5 62.8 %collective-permute-start.8 = (bf16[384,768]{1,0:T(8,128)(2,1)}, bf16[384,768]{1,0:T(8,128)(2,1)S(1)}, u32[]{:S(2)}, u32[]{:S(2)}) collective-permute-start(bf16[384,768]{1,0:T(8,128)(2,1)} %get-tuple-element.19), channel_id=1, source_target_pairs={{0,1},{1,0},{2,3},{3,2},{4,5},{5,4},{6,7},{7,6},{8,9},{9,8},{10,11... | collective-permute-start | bytes 1769480 | tf_op jit(solution)/shard_map/ppermute | solution.py:17
  16.5 3.6 %copy-start.22 = (f32[256]{0:T(256)}, f32[256]{0:T(256)S(1)}, u32[]{:S(2)}) copy-start(f32[256]{0:T(256)S(1)} %broadcast_multiply_fusion.8) | copy-start | bytes 3076
  17.0 3.0 %copy-start.26 = (f32[256]{0:T(256)}, f32[256]{0:T(256)S(1)}, u32[]{:S(2)}) copy-start(f32[256]{0:T(256)S(1)} %add_rsqrt_fusion.6) | copy-start | bytes 3076
  18.1 2.5 %copy-start.11 = (bf16[1,384,1536]{2,1,0:T(8,128)(2,1)S(1)}, bf16[1,384,1536]{2,1,0:T(8,128)(2,1)}, u32[]{:S(2)}) copy-start(bf16[1,384,1536]{2,1,0:T(8,128)(2,1)} %param.13) | copy-start | bytes 3538948
  20.0 27.6 %copy-start.4 = (bf16[1,256,3072]{2,1,0:T(8,128)(2,1)S(1)}, bf16[1,256,3072]{2,1,0:T(8,128)(2,1)}, u32[]{:S(2)}) copy-start(bf16[1,256,3072]{2,1,0:T(8,128)(2,1)} %param.11) | copy-start | bytes 4718596
  20.0 114.3 %collective-permute-start = (bf16[256,3072]{1,0:T(8,128)(2,1)}, bf16[256,3072]{1,0:T(8,128)(2,1)}, u32[]{:S(2)}, u32[]{:S(2)}) collective-permute-start(bf16[256,3072]{1,0:T(8,128)(2,1)} %fusion.8), channel_id=1, source_target_pairs={{0,1},{1,0},{2,3},{3,2},{4,5},{5,4},{6,7},{7,6},{8,9},{9,8},{10,11... | collective-permute-start | bytes 4718600 | tf_op jit(solution)/shard_map/ppermute | solution.py:17
  21.6 139.2 %collective-permute-start.10 = (bf16[384,768]{1,0:T(8,128)(2,1)}, bf16[384,768]{1,0:T(8,128)(2,1)}, u32[]{:S(2)}, u32[]{:S(2)}) collective-permute-start(bf16[384,768]{1,0:T(8,128)(2,1)} %get-tuple-element.24), channel_id=1, source_target_pairs={{0,1},{1,0},{2,3},{3,2},{4,5},{5,4},{6,7},{7,6},{8,9},{9,8},{10,11... | collective-permute-start | bytes 1769480 | tf_op jit(solution)/shard_map/ppermute | solution.py:17
  42.1 28.9 %collective-permute-start.3 = (bf16[384,768]{1,0:T(8,128)(2,1)}, bf16[384,768]{1,0:T(8,128)(2,1)}, u32[]{:S(2)}, u32[]{:S(2)}) collective-permute-start(bf16[384,768]{1,0:T(8,128)(2,1)} %collective-permute-done.1), channel_id=1, source_target_pairs={{0,2},{2,4},{4,6},{6,8},{8,10},{10,12},{12,14},{14,0},{1,3},{3,5},... | collective-permute-start | bytes 1769480 | tf_op jit(solution)/shard_map/ppermute | solution.py:43
  44.6 29.6 %collective-permute-start.4 = (bf16[384,768]{1,0:T(8,128)(2,1)S(1)}, bf16[384,768]{1,0:T(8,128)(2,1)}, u32[]{:S(2)}, u32[]{:S(2)}) collective-permute-start(bf16[384,768]{1,0:T(8,128)(2,1)S(1)} %collective-permute-done.2), channel_id=1, source_target_pairs={{0,14},{2,0},{4,2},{6,4},{8,6},{10,8},{12,10},{14,12},{1,15},{3,1}... | collective-permute-start | bytes 1769480 | tf_op jit(solution)/shard_map/ppermute | solution.py:46
  71.0 39.2 %collective-permute-start.5 = (bf16[384,768]{1,0:T(8,128)(2,1)}, bf16[384,768]{1,0:T(8,128)(2,1)S(1)}, u32[]{:S(2)}, u32[]{:S(2)}) collective-permute-start(bf16[384,768]{1,0:T(8,128)(2,1)} %collective-permute-done.3), channel_id=1, source_target_pairs={{0,2},{2,4},{4,6},{6,8},{8,10},{10,12},{12,14},{14,0},{1,3},{3,5},... | collective-permute-start | bytes 1769480 | tf_op jit(solution)/shard_map/ppermute | solution.py:43
  72.9 5.4 %copy-start.5 = (bf16[256,3072]{1,0:T(8,128)(2,1)S(1)}, bf16[256,3072]{1,0:T(8,128)(2,1)}, u32[]{:S(2)}) copy-start(bf16[256,3072]{1,0:T(8,128)(2,1)} %fusion.22) | copy-start | bytes 4718596
  74.2 53.0 %collective-permute-start.6 = (bf16[384,768]{1,0:T(8,128)(2,1)}, bf16[384,768]{1,0:T(8,128)(2,1)S(1)}, u32[]{:S(2)}, u32[]{:S(2)}) collective-permute-start(bf16[384,768]{1,0:T(8,128)(2,1)} %collective-permute-done.4), channel_id=1, source_target_pairs={{0,14},{2,0},{4,2},{6,4},{8,6},{10,8},{12,10},{14,12},{1,15},{3,1}... | collective-permute-start | bytes 1769480 | tf_op jit(solution)/shard_map/ppermute | solution.py:46
  78.3 76.5 %collective-permute-start.9 = (bf16[256,3072]{1,0:T(8,128)(2,1)S(1)}, bf16[256,3072]{1,0:T(8,128)(2,1)}, u32[]{:S(2)}, u32[]{:S(2)}) collective-permute-start(bf16[256,3072]{1,0:T(8,128)(2,1)S(1)} %copy-done.5), channel_id=1, source_target_pairs={{0,1},{1,0},{2,3},{3,2},{4,5},{5,4},{6,7},{7,6},{8,9},{9,8},{10,11... | collective-permute-start | bytes 4718600 | tf_op jit(solution)/shard_map/ppermute | solution.py:17
  110.2 24.1 %collective-permute-start.7 = (bf16[384,768]{1,0:T(8,128)(2,1)S(1)}, bf16[384,768]{1,0:T(8,128)(2,1)S(1)}, u32[]{:S(2)}, u32[]{:S(2)}) collective-permute-start(bf16[384,768]{1,0:T(8,128)(2,1)S(1)} %collective-permute-done.5), channel_id=1, source_target_pairs={{0,2},{2,4},{4,6},{6,8},{8,10},{10,12},{12,14},{14,0},{1,3},{3,5},... | collective-permute-start | bytes 1769480 | tf_op jit(solution)/shard_map/ppermute | solution.py:43
  134.3 6.2 %copy-start.3 = (bf16[3072,768]{1,0:T(8,128)(2,1)}, bf16[3072,768]{1,0:T(8,128)(2,1)S(1)}, u32[]{:S(2)}) copy-start(bf16[3072,768]{1,0:T(8,128)(2,1)S(1)} %constant_dynamic-update-slice_fusion) | copy-start | bytes 14155780
  140.6 11.9 %copy-start.1 = (f32[512,768]{1,0:T(8,128)}, f32[512,768]{1,0:T(8,128)S(1)}, u32[]{:S(2)}) copy-start(f32[512,768]{1,0:T(8,128)S(1)} %fusion.14) | copy-start | bytes 4718596
  141.1 2.4 %copy-start.20 = (f32[512]{0:T(512)}, f32[512]{0:T(512)S(1)}, u32[]{:S(2)}) copy-start(f32[512]{0:T(512)S(1)} %get-tuple-element.57) | copy-start | bytes 6148
  141.1 9.1 %copy-start.14 = (f32[512]{0:T(512)}, f32[512]{0:T(512)S(1)}, u32[]{:S(2)}) copy-start(f32[512]{0:T(512)S(1)} %get-tuple-element.56) | copy-start | bytes 6148
  141.1 11.3 %copy-start.28 = (f32[512]{0:T(512)}, f32[512]{0:T(512)S(1)}, u32[]{:S(2)}) copy-start(f32[512]{0:T(512)S(1)} %get-tuple-element.52) | copy-start | bytes 6148
  143.5 4.5 %copy-start.16 = (f32[512]{0:T(512)}, f32[512]{0:T(512)S(1)}, u32[]{:S(2)}) copy-start(f32[512]{0:T(512)S(1)} %get-tuple-element.54) | copy-start | bytes 6148
  143.5 4.5 %copy-start.18 = (f32[512]{0:T(512)}, f32[512]{0:T(512)S(1)}, u32[]{:S(2)}) copy-start(f32[512]{0:T(512)S(1)} %get-tuple-element.55) | copy-start | bytes 6148
  154.7 6.1 %copy-start.13 = (bf16[384,768]{1,0:T(8,128)(2,1)S(1)}, bf16[384,768]{1,0:T(8,128)(2,1)}, u32[]{:S(2)}) copy-start(bf16[384,768]{1,0:T(8,128)(2,1)} %get-tuple-element.25) | copy-start | bytes 1769476
  154.7 6.1 %copy-start.10 = (f32[512,768]{1,0:T(8,128)S(1)}, f32[512,768]{1,0:T(8,128)}, u32[]{:S(2)}) copy-start(f32[512,768]{1,0:T(8,128)} %get-tuple-element.27) | copy-start | bytes 4718596
  160.8 1.4 copy-start.25
  162.3 1.4 copy-start.9
  165.0 1.4 copy-start.8
  165.0 1.4 copy-start.32
  167.8 1.4 copy-start.7
  167.8 1.4 copy-start.31
  170.6 1.4 copy-start.6
  170.6 1.4 copy-start.30
  173.4 1.4 copy-start.35
  173.4 1.4 copy-start.36
  174.8 1.8 copy-start.2
  174.8 1.8 copy-start.15
  174.8 1.8 copy-start.17
  174.8 1.8 copy-start.19
  174.8 1.8 copy-start.21
  174.8 1.8 copy-start.29
  174.8 4.5 %slice-start = ((s8[4718592]{0:T(1024)(128)(4,1)}), s8[4194304]{0:T(1024)(128)(4,1)S(1)}, s32[]{:S(2)}) async-start(s8[4718592]{0:T(1024)(128)(4,1)} %bitcast.57), calls=%async_computation.1 | async-start | bytes 8388608
  176.6 2.8 %slice-start.1 = ((s8[4718592]{0:T(1024)(128)(4,1)}), s8[524288]{0:T(1024)(128)(4,1)S(1)}, s32[]{:S(2)}) async-start(s8[4718592]{0:T(1024)(128)(4,1)} %bitcast.57), calls=%async_computation.2 | async-start | bytes 1048576
  179.4 4.9 %copy-start.23 = (f32[256]{0:T(256)S(1)}, f32[256]{0:T(256)}, u32[]{:S(2)}) copy-start(f32[256]{0:T(256)} %copy-done.22) | copy-start | bytes 3076
  179.4 4.9 %copy-start.27 = (f32[256]{0:T(256)S(1)}, f32[256]{0:T(256)}, u32[]{:S(2)}) copy-start(f32[256]{0:T(256)} %copy-done.26) | copy-start | bytes 3076
  180.8 3.5 %collective-permute-start.11 = (bf16[256,3072]{1,0:T(8,128)(2,1)S(1)}, bf16[256,3072]{1,0:T(8,128)(2,1)S(1)}, u32[]{:S(2)}, u32[]{:S(2)}) collective-permute-start(bf16[256,3072]{1,0:T(8,128)(2,1)S(1)} %convolution_convert_fusion), channel_id=1, source_target_pairs={{0,1},{1,0},{2,3},{3,2},{4,5},{5,4},{6,7},{7,6},{8,9},{9,8},{10,11... | collective-permute-start | bytes 4718600 | tf_op jit(solution)/shard_map/ppermute | solution.py:17
  (4 other events, 4.6 us)
Sparse Core Ops, SparseCore 0:
  9.4 142.0 all-gather.1
